TPU v7x, 32 devices: a whole 2x2x4 slice. The times are simulated.
32 devices in a mesh: replica: 16 (over z, y, x), tensor: 2 (over core).
Axes of the slice: x: 2, y: 2, z: 4, core: 2. Of those that a mesh axis runs over, the one named last changes fastest.
Arguments:
- queries: bfloat16 [2048, 4096], P('replica', 'tensor'), may hold values from -9 to 9
- new_kv: bfloat16 [2, 2048, 1024], P(None, 'replica', 'tensor'), may hold values from -16 to 16
- cache: bfloat16 [128, 2, 64, 1024], P('replica', None, None, 'tensor'), may hold values from -16 to 16
- block_owner: int32 [16, 64], replicated, may hold values from 0 to 15, as said below
- block_slot: int32 [16, 64], replicated, may hold values from 0 to 7, as said below
- prefix_blocks: int32 [16], replicated, may hold values from 1 to 64, 512 in all
- out_weight: bfloat16 [4096, 4096], P('tensor'), may hold values from -0.09375 to 0.09375
Outputs:
- mixed: bfloat16 [2048, 4096], P(('replica', 'tensor'))
Inputs may be any that keep to these rules, and one draw needn't show every extreme that they name: `block_owner`: within one replica's row, every owner that appears does so exactly 4 times. `block_slot`: the 4 entries of one replica's row that name one owner name different slots. `prefix_blocks`: the largest is 64 in every draw.
All inputs are finite; a program needn't handle non-finite values.
Results may differ from a plain program's by a relative error of at most 0.024.
Values may be sent and summed in bfloat16 or wider, within the bound.
A program may use at most 128 MiB of HBM per device.

v0:
```python
import jax
import jax.numpy as jnp
from jax import lax
from jax.sharding import PartitionSpec as P

HQ = 32
KVH = 8
HD = 128
BLOCK = 64
MAXB = 64


NEGATIVE = -1e30


def tile_update(softmax_state, query_heads, key_rows, value_rows, allowed, scaling):
    running, totals, weighted = softmax_state
    scores = (
        jnp.einsum("tkgd,skd->kgts", query_heads, key_rows, preferred_element_type=jnp.float32)
        * scaling
    )
    scores = jnp.where(allowed, scores, NEGATIVE)
    fresh = jnp.maximum(running, jnp.max(scores, axis=3))
    weights = jnp.where(allowed, jnp.exp(scores - fresh[..., None]), 0.0)
    factor = jnp.exp(running - fresh)
    totals = totals * factor + jnp.sum(weights, axis=3)
    increment = jnp.einsum(
        "kgts,skd->tkgd",
        weights.astype(jnp.bfloat16),
        value_rows,
        preferred_element_type=jnp.float32,
    )
    weighted = weighted * jnp.transpose(factor, (2, 0, 1))[..., None] + increment
    return (fresh, totals, weighted)


def fold_range(
    softmax_state, query_heads, key_rows, value_rows, lower_key, upper_key, key_span, scaling
):
    tile_first = lower_key // key_span
    tile_last = (upper_key + key_span - 1) // key_span

    def advance(position, carried):
        offset = position * key_span
        key_tile = lax.dynamic_slice_in_dim(key_rows, offset, key_span, 0)
        value_tile = lax.dynamic_slice_in_dim(value_rows, offset, key_span, 0)
        places = offset + jnp.arange(key_span, dtype=jnp.int32)
        allowed = ((places >= lower_key) & (places < upper_key))[None, None, None, :]
        return tile_update(carried, query_heads, key_tile, value_tile, allowed, scaling)

    return lax.fori_loop(tile_first, tile_last, advance, softmax_state)


def fold_blocks(
    softmax_state, query_heads, arrived, positions, lower_block, upper_block, key_span, scaling
):
    chosen = arrived[positions]
    block_len = chosen.shape[2]
    key_count = chosen.shape[0] * block_len
    heads_kv = query_heads.shape[1]
    key_rows = chosen[:, 0].reshape(key_count, heads_kv, -1)
    value_rows = chosen[:, 1].reshape(key_count, heads_kv, -1)
    return fold_range(
        softmax_state,
        query_heads,
        key_rows,
        value_rows,
        lower_block * block_len,
        upper_block * block_len,
        key_span,
        scaling,
    )


def suffix_pass(softmax_state, query_heads, new_keys, new_values, key_span, scaling):
    key_count = new_keys.shape[0]
    row_ids = jnp.arange(key_count, dtype=jnp.int32)
    columns = 0 + jnp.arange(key_span, dtype=jnp.int32)
    allowed = (row_ids[:, None] >= columns[None, :])[None, None]
    softmax_state = tile_update(softmax_state, query_heads, new_keys, new_values, allowed, scaling)
    return softmax_state


def send_table(owner_rows, slot_rows, lower, upper, own_index, capacity):
    places = jnp.arange(owner_rows.shape[1], dtype=jnp.int32)
    chosen = (
        (owner_rows == own_index)
        & (places[None, :] >= lower[:, None])
        & (places[None, :] < upper[:, None])
    )
    ranks = jnp.cumsum(chosen.astype(jnp.int32), axis=1) - 1
    levels = jnp.arange(capacity, dtype=jnp.int32)
    matches = chosen[:, None, :] & (ranks[:, None, :] == levels[None, :, None])
    return jnp.sum(jnp.where(matches, slot_rows[:, None, :] + 1, 0), axis=2)


def receive_index(owner_row, lower, upper, capacity, lane, lane_count):
    places = jnp.arange(owner_row.shape[0], dtype=jnp.int32)
    chosen = (places >= lower) & (places < upper)
    same_owner = owner_row[:, None] == owner_row[None, :]
    earlier = places[None, :] < places[:, None]
    ranks = jnp.sum((same_owner & earlier & chosen[None, :]).astype(jnp.int32), axis=1)
    spots = owner_row * (capacity * lane_count) + lane * capacity + ranks
    return jnp.where(chosen, spots, 0)


def local(queries, new_kv, cache, block_owner, block_slot, prefix_blocks, out_weight):
    replicas = lax.axis_size("replica")
    own_index = lax.axis_index("replica")
    capacity = max(2, MAXB // replicas)
    tokens = queries.shape[0]
    heads_kv = cache.shape[3] // HD
    per_group = HQ // KVH
    scaling = HD ** (-0.5)
    key_span = min(512, MAXB // 2 * BLOCK)
    query_heads = queries.reshape(tokens, heads_kv, per_group, HD)
    new_keys = new_kv[0].reshape(tokens, heads_kv, HD)
    new_values = new_kv[1].reshape(tokens, heads_kv, HD)
    blank_state = (
        jnp.full((heads_kv, per_group, tokens), NEGATIVE, jnp.float32),
        jnp.zeros((heads_kv, per_group, tokens), jnp.float32),
        jnp.zeros((tokens, heads_kv, per_group, HD), jnp.float32),
    )
    nothing = jnp.zeros((), jnp.int32)
    own_row = lax.dynamic_index_in_dim(block_owner, own_index, 0, keepdims=False)
    own_length = lax.dynamic_index_in_dim(prefix_blocks, own_index, 0, keepdims=False)
    slot_table = send_table(
        block_owner, block_slot, jnp.zeros_like(prefix_blocks), prefix_blocks, own_index, capacity
    )[:, None]
    lane_count = 1
    keep_index = receive_index(own_row, nothing, own_length, capacity, 0, lane_count)
    requested = slot_table.reshape(-1)
    picked = cache[jnp.maximum(requested - 1, 0)]
    picked = picked.reshape((replicas, lane_count * capacity) + cache.shape[1:])
    arrived = lax.all_to_all(picked, "replica", split_axis=0, concat_axis=0, tiled=True)
    arrived = arrived.reshape((replicas * lane_count * capacity,) + cache.shape[1:])
    softmax_state = suffix_pass(
        blank_state, query_heads, new_keys, new_values, min(512, tokens), scaling
    )
    softmax_state = fold_blocks(
        softmax_state, query_heads, arrived, keep_index, nothing, own_length, key_span, scaling
    )
    attention = softmax_state[2] / jnp.transpose(softmax_state[1], (2, 0, 1))[..., None]
    attention = attention.reshape(tokens, heads_kv * per_group * HD).astype(jnp.bfloat16)
    return lax.psum_scatter(
        jnp.dot(attention, out_weight, preferred_element_type=jnp.float32).astype(jnp.bfloat16),
        "tensor",
        scatter_dimension=0,
        tiled=True,
    )


def solution(mesh):
    placed = (
        P("replica", "tensor"),
        P(None, "replica", "tensor"),
        P("replica", None, None, "tensor"),
        P(),
        P(),
        P(),
        P("tensor", None),
    )
    return jax.shard_map(
        local, mesh=mesh, in_specs=placed, out_specs=P(("replica", "tensor"), None), check_vma=False
    )
```

profile of v0, /device:TPU:11, one launch (start us, length us, event | category | flops | bytes accessed | tf_op | source)
XLA Modules:
  0.0 343.4 jit_solution(10866783051780195672)
XLA Ops:
  6.5 0.9 fusion.41
  7.6 0.7 broadcast_add_fusion
  8.7 5.4 %gather_fusion = bf16[64,2,64,512]{3,2,1,0:T(8,128)(2,1)} fusion(bf16[8,2,64,512]{3,2,1,0:T(8,128)(2,1)S(1)} %copy-done, s32[1024]{0:T(1024)S(1)} %pad_clamp_fusion.1), kind=kCustom, calls=%fused_computation | custom fusion | bytes 16777472 | tf_op jit(solution)/shard_map/gather | solution.py:133
  14.1 6.8 %all-to-all-start = ((bf16[16,4,2,64,512]{4,3,2,1,0:T(8,128)(2,1)}), bf16[16,4,2,64,512]{4,3,2,1,0:T(8,128)(2,1)}, u32[]{:S(2)}, u32[]{:S(2)}) async-start(bf16[16,4,2,64,512]{4,3,2,1,0:T(8,128)(2,1)} %bitcast.115), calls=%async_computation | async-start | bytes 16777216 | tf_op jit(solution)/shard_map/all_to_all | solution.py:135
  20.9 0.6 dynamic_slice.14
  23.0 0.4 fusion.45
  23.6 1.5 fusion.23
  25.1 1.6 copy.32
  26.7 0.6 iota_compare_fusion.4
  27.3 0.7 fusion.39
  28.2 1.3 fusion.38
  29.5 179.0 %all-to-all-done = bf16[16,4,2,64,512]{4,3,2,1,0:T(8,128)(2,1)} async-done(((bf16[16,4,2,64,512]{4,3,2,1,0:T(8,128)(2,1)}), bf16[16,4,2,64,512]{4,3,2,1,0:T(8,128)(2,1)}, u32[]{:S(2)}, u32[]{:S(2)}) %all-to-all-start) | async-done | bytes 8388640 | tf_op jit(solution)/shard_map/all_to_all | solution.py:135
  208.5 8.8 %gather_fusion.1 = bf16[64,2,64,512]{3,2,1,0:T(8,128)(2,1)} fusion(bf16[64,2,64,512]{3,2,1,0:T(8,128)(2,1)} %bitcast.17, s32[1024]{0:T(1024)S(1)} %pad_clamp_fusion), kind=kCustom, calls=%fused_computation.1 | custom fusion | bytes 16777472 | tf_op jit(solution)/shard_map/gather | solution.py:57
  217.3 6.0 %fusion.43 = (bf16[64,1,64,512]{3,2,1,0:T(8,128)(2,1)}, bf16[64,1,64,512]{3,2,1,0:T(8,128)(2,1)}) fusion(bf16[64,2,64,512]{3,2,1,0:T(8,128)(2,1)} %gather_fusion.1), kind=kLoop, calls=%fused_computation.70 | loop fusion | bytes 16777216 | tf_op jit(solution)/shard_map/slice | solution.py:62
  223.3 6.9 %reshape_squeeze.14 = bf16[4096,4,128]{2,1,0:T(4,128)(2,1)} reshape(bf16[64,1,64,512]{3,2,1,0:T(8,128)(2,1)} %get-tuple-element.110) | data formatting | bytes 8388608 | tf_op jit(solution)/shard_map/reshape;squeeze | solution.py:61
  230.2 6.9 %reshape_squeeze.15 = bf16[4096,4,128]{2,1,0:T(4,128)(2,1)} reshape(bf16[64,1,64,512]{3,2,1,0:T(8,128)(2,1)} %get-tuple-element.109) | data formatting | bytes 8388608 | tf_op jit(solution)/shard_map/reshape;squeeze | solution.py:62
  237.1 29.1 %while.14 = (s32[]{:T(128)}, f32[4,4,128]{2,1,0:T(4,128)S(1)}, f32[4,4,128]{2,1,0:T(4,128)S(1)}, f32[128,4,4,128]{0,3,2,1:T(8,128)S(1)}, s32[]{:T(128)}, /*index...) while((s32[]{:T(128)}, f32[4,4,128]{2,1,0:T(4,128)S(1)}, ...), condition=%wide.region_8.9_spmd, body=%wide.region_5.8_spmd.sunk | while | flops 551034880 | bytes 36309200 | solution.py:51
  237.1 1.6 constant_dynamic-slice_fusion.4
  238.7 2.7 bitcast_reduce_fusion.2
  241.8 3.8 %fusion.65 = f32[128,4,4,128]{0,3,2,1:T(8,128)S(1)} fusion(f32[4,512,128,4]{2,1,3,0:T(8,128)} %get-tuple-element.184, f32[4,4,128]{2,1,0:T(4,128)S(1)} %get-tuple-element.214, pred[512]{0:T(512)(128)(4,1)S(1)} %fusion.62, f32[128,4,4,128]{0,3,2,1:T(8,128)S(1)} %get-tuple-element.203, bf16[512,4,128]{0,2,1:T(8,128)(2,1)S(1)} %copy.58, ...), kind=kOutput, calls=%fused_computation.13.clone.1 | convolution fusion | flops 274202624 | bytes 6832640 | tf_op jit(solution)/shard_map/while/body/kgts,skd->tkgd/dot_general | solution.py:27
  245.5 1.2 fusion.64
  246.7 1.6 constant_dynamic-slice_fusion.4
  248.3 2.7 bitcast_reduce_fusion.2
  251.4 3.8 %fusion.65 = f32[128,4,4,128]{0,3,2,1:T(8,128)S(1)} fusion(f32[4,512,128,4]{2,1,3,0:T(8,128)} %get-tuple-element.184, f32[4,4,128]{2,1,0:T(4,128)S(1)} %get-tuple-element.214, pred[512]{0:T(512)(128)(4,1)S(1)} %fusion.62, f32[128,4,4,128]{0,3,2,1:T(8,128)S(1)} %get-tuple-element.203, bf16[512,4,128]{0,2,1:T(8,128)(2,1)S(1)} %copy.58, ...), kind=kOutput, calls=%fused_computation.13.clone.1 | convolution fusion | flops 274202624 | bytes 6832640 | tf_op jit(solution)/shard_map/while/body/kgts,skd->tkgd/dot_general | solution.py:27
  255.2 1.2 fusion.64
  256.4 1.6 constant_dynamic-slice_fusion.4
  258.0 2.7 bitcast_reduce_fusion.2
  260.7 0.3 copy.58
  261.1 3.8 %fusion.65 = f32[128,4,4,128]{0,3,2,1:T(8,128)S(1)} fusion(f32[4,512,128,4]{2,1,3,0:T(8,128)} %get-tuple-element.184, f32[4,4,128]{2,1,0:T(4,128)S(1)} %get-tuple-element.214, pred[512]{0:T(512)(128)(4,1)S(1)} %fusion.62, f32[128,4,4,128]{0,3,2,1:T(8,128)S(1)} %get-tuple-element.203, bf16[512,4,128]{0,2,1:T(8,128)(2,1)S(1)} %copy.58, ...), kind=kOutput, calls=%fused_computation.13.clone.1 | convolution fusion | flops 274202624 | bytes 6832640 | tf_op jit(solution)/shard_map/while/body/kgts,skd->tkgd/dot_general | solution.py:27
  264.8 1.2 fusion.64
  266.4 9.2 %convolution_convert_fusion = bf16[128,4096]{1,0:T(8,128)(2,1)} fusion(bf16[128,2048]{0,1:T(8,128)(2,1)S(1)} %bitcast.119, bf16[2048,4096]{1,0:T(8,128)(2,1)} %param.15), kind=kOutput, calls=%fused_computation.29 | convolution fusion | flops 2148007936 | bytes 18350080 | tf_op jit(solution)/shard_map/dot_general | solution.py:146
  275.6 60.9 %reduce-scatter.2.cloned.1.call-done = bf16[64,4096]{1,0:T(8,128)(2,1)} async-done(((bf16[128,4096]{1,0:T(8,128)(2,1)}), bf16[64,4096]{1,0:T(8,128)(2,1)}) %reduce-scatter.2.cloned.1.call-update) | async-done | bytes 524304 | tf_op jit(solution)/shard_map/reduce_scatter | solution.py:145
  (50 shorter events, 2.7 us)
Async XLA Ops:
  6.5 2.2 copy-start
  14.1 6.8 %copy-start.5 = (s32[16]{0:T(128)S(1)}, s32[16]{0:T(128)}, u32[]{:S(2)}) copy-start(s32[16]{0:T(128)} %param.14) | copy-start | bytes 196
  14.1 8.0 %copy-start.3 = (bf16[128,2048]{1,0:T(8,128)(2,1)S(1)}, bf16[128,2048]{1,0:T(8,128)(2,1)}, u32[]{:S(2)}) copy-start(bf16[128,2048]{1,0:T(8,128)(2,1)} %param.9) | copy-start | bytes 1572868
  14.1 8.3 %copy-start.4 = (bf16[2,128,512]{2,1,0:T(8,128)(2,1)S(1)}, bf16[2,128,512]{2,1,0:T(8,128)(2,1)}, u32[]{:S(2)}) copy-start(bf16[2,128,512]{2,1,0:T(8,128)(2,1)} %param.10) | copy-start | bytes 786436
  14.1 194.4 %all-to-all-start = ((bf16[16,4,2,64,512]{4,3,2,1,0:T(8,128)(2,1)}), bf16[16,4,2,64,512]{4,3,2,1,0:T(8,128)(2,1)}, u32[]{:S(2)}, u32[]{:S(2)}) async-start(bf16[16,4,2,64,512]{4,3,2,1,0:T(8,128)(2,1)} %bitcast.115), calls=%async_computation | async-start | bytes 16777216 | tf_op jit(solution)/shard_map/all_to_all | solution.py:135
  20.9 315.6 %reduce-scatter.2.cloned.1.call-start = ((), (), s32[]{:S(2)}) async-start(), calls=%async_computation.2 | async-start | bytes 1572864 | tf_op jit(solution)/shard_map/reduce_scatter | solution.py:145
  241.8 3.8 %copy-start.2 = (f32[4,512,128,4]{2,1,3,0:T(8,128)S(1)}, f32[4,512,128,4]{2,1,3,0:T(8,128)}, u32[]{:S(2)}) copy-start(f32[4,512,128,4]{2,1,3,0:T(8,128)} %get-tuple-element.184) | copy-start | bytes 12582916 | tf_op jit(solution)/shard_map/while
  251.4 3.8 %copy-start.2 = (f32[4,512,128,4]{2,1,3,0:T(8,128)S(1)}, f32[4,512,128,4]{2,1,3,0:T(8,128)}, u32[]{:S(2)}) copy-start(f32[4,512,128,4]{2,1,3,0:T(8,128)} %get-tuple-element.184) | copy-start | bytes 12582916 | tf_op jit(solution)/shard_map/while
  261.1 3.8 %copy-start.2 = (f32[4,512,128,4]{2,1,3,0:T(8,128)S(1)}, f32[4,512,128,4]{2,1,3,0:T(8,128)}, u32[]{:S(2)}) copy-start(f32[4,512,128,4]{2,1,3,0:T(8,128)} %get-tuple-element.184) | copy-start | bytes 12582916 | tf_op jit(solution)/shard_map/while
  266.4 70.2 %copy-start.1 = (bf16[8,2,64,512]{3,2,1,0:T(8,128)(2,1)S(1)}, bf16[8,2,64,512]{3,2,1,0:T(8,128)(2,1)}, u32[]{:S(2)}) copy-start(bf16[8,2,64,512]{3,2,1,0:T(8,128)(2,1)} %param.11) | copy-start | bytes 3145732
Sparse Core Ops, SparseCore 0:
  275.8 60.7 reduce-scatter.1
where the time goes:
time: 344 us; the launch traced here: 343 us
  waiting for transfers between devices  240 us (70%)
  local copies, waits for them, and re-layouts  43.6 us (13%)
  matrix products  30.6 us (9%)
  between operations  14.1 us (4%)
  other arithmetic  7.93 us (2%)
  starting transfers between devices  6.79 us (2%)
    all_to_all x1, waiting for transfers between devices, local(): lax.all_to_all(picked, 'replica', split_axis=0, concat_axis=0, tiled=True)  179 us
    reduce_scatter x1, waiting for transfers between devices, local(): lax.psum_scatter(jnp.dot(attention, out_weight, preferred_element_type=jn...  60.9 us
    dot_general x4, matrix products, tile_update(): jnp.einsum('kgts,skd->tkgd', weights.astype(jnp.bfloat16), value_rows, pr...  12.8 us
    dot_general x1, matrix products, local(): jnp.dot(attention, out_weight, preferred_element_type=jnp.float32)  9.24 us
    gather x1, local copies, waits for them, and re-layouts, fold_blocks(): chosen = arrived[positions]  8.82 us
    dot_general x4, matrix products, tile_update(): jnp.einsum('tkgd,skd->kgts', query_heads, key_rows, preferred_element_typ...  8.58 us
    another operation x1, local copies, waits for them, and re-layouts, fold_blocks(): key_rows = chosen[:, 0].reshape(key_count, heads_kv, -1)  6.93 us
    another operation x1, local copies, waits for them, and re-layouts, fold_blocks(): value_rows = chosen[:, 1].reshape(key_count, heads_kv, -1)  6.92 us
  transfers between devices with their start and end apart: 2, of which 2 were waited for; matrix products, arithmetic and copies ran while one was open for 2% of the time, Pallas kernels for 0%

commit v1 on v0

v1 whole, which is shorter than its diff:
```python
import functools
import math

import jax
import jax.numpy as jnp
from jax import lax
from jax.experimental import pallas as pl
from jax.experimental.pallas import tpu as pltpu
from jax.sharding import PartitionSpec as P

HQ = 32
KVH = 8
HD = 128
BLOCK = 64
MAXB = 64
PER_GROUP = HQ // KVH

FLOOR = -1e29
MASKED = -2e30
MESH = pl.DeviceIdType.MESH


def block_tables(block_owner, block_slot, prefix_blocks, own, planes, members, capacity):
    plane, member = own // members, own % members
    rows = ((plane + jnp.arange(planes, dtype=jnp.int32)) % planes) * members + member
    owners = plane * members + (member + jnp.arange(members, dtype=jnp.int32)) % members
    places = jnp.arange(block_owner.shape[1], dtype=jnp.int32)
    owner_rows, slot_rows, lengths = block_owner[rows], block_slot[rows], prefix_blocks[rows]
    used = places[None, :] < lengths[:, None]
    chosen = (owner_rows[:, None, :] == owners[None, :, None]) & used[:, None, :]
    ranks = jnp.cumsum(chosen.astype(jnp.int32), axis=2) - 1
    levels = jnp.arange(capacity, dtype=jnp.int32)
    matches = chosen[:, :, None, :] & (ranks[:, :, None, :] == levels[None, None, :, None])
    slots = jnp.sum(jnp.where(matches, slot_rows[:, None, None, :], 0), axis=3)
    return slots.reshape(-1), jnp.sum(chosen.astype(jnp.int32), axis=2).reshape(-1)


def attend_kernel(
    planes, members, capacity, slots_ref, counts_ref, q_ref, new_ref, cache_ref, out_ref,
    qbuf, kvbuf, acc, stat, part_out, part_in, stat_in,
    q_send, q_recv, kv_send, kv_recv, p_send, p_recv, s_send, s_recv,
):
    own = lax.axis_index("replica")
    plane, member = lax.div(own, members), lax.rem(own, members)
    heads_kv, lanes = acc.shape[1], acc.shape[3]
    tokens = lanes // PER_GROUP
    factor = HD ** (-0.5) * math.log2(math.e)

    def column(i):
        return {"replica": lax.rem(plane + i, planes) * members + member}

    def in_plane(j):
        return {"replica": plane * members + lax.rem(member + j, members)}

    def q_copy(i):
        return pltpu.make_async_remote_copy(
            qbuf.at[0], qbuf.at[planes - i], q_send.at[i], q_recv.at[planes - i],
            device_id=column(i), device_id_type=MESH)

    def kv_copy(j):
        return pltpu.make_async_remote_copy(
            cache_ref, kvbuf[members - j - 1], kv_send.at[j], kv_recv.at[members - j],
            device_id=in_plane(j), device_id_type=MESH)

    def part_copy(i):
        return pltpu.make_async_remote_copy(
            part_out.at[i], part_in.at[planes - i], p_send.at[i], p_recv.at[planes - i],
            device_id=column(i), device_id_type=MESH)

    def stat_copy(i):
        return pltpu.make_async_remote_copy(
            stat.at[i], stat_in.at[planes - i], s_send.at[i], s_recv.at[planes - i],
            device_id=column(i), device_id_type=MESH)

    barrier = pltpu.get_barrier_semaphore()
    for i in range(1, planes):
        pl.semaphore_signal(barrier, inc=1, device_id=column(i), device_id_type=MESH)
    for j in range(1, members):
        pl.semaphore_signal(barrier, inc=1, device_id=in_plane(j), device_id_type=MESH)
    for head in range(heads_kv * PER_GROUP):
        k, g = divmod(head, PER_GROUP)
        qbuf[0, k, g * tokens:(g + 1) * tokens, :] = q_ref[:, head * HD:(head + 1) * HD]
    pl.semaphore_wait(barrier, planes + members - 2)

    for i in range(1, planes):
        q_copy(i).start()
    for j in range(1, members):
        kv_copy(j).start()

    def update(i, k, keys, values, allowed):
        scores = lax.dot_general(
            keys, qbuf[i, k], (((1,), (1,)), ((), ())), preferred_element_type=jnp.float32)
        scores = jnp.where(allowed, scores * factor, MASKED)
        before = stat[i, k:k + 1, :]
        highest = jnp.maximum(before, jnp.max(scores, axis=0, keepdims=True))
        weights = jnp.exp2(scores - highest)
        scale = jnp.exp2(before - highest)
        total = stat[i, heads_kv + k:heads_kv + k + 1, :]
        stat[i, heads_kv + k:heads_kv + k + 1, :] = (
            total * scale + jnp.sum(weights, axis=0, keepdims=True))
        stat[i, k:k + 1, :] = highest
        acc[i, k] = acc[i, k] * scale + lax.dot_general(
            values, weights.astype(jnp.bfloat16), (((0,), (0,)), ((), ())),
            preferred_element_type=jnp.float32)

    def fold(i, j):
        source = cache_ref if j == 0 else kvbuf[j - 1]
        pair = i * members + j
        slots = [slots_ref[pair * capacity + c] for c in range(capacity)]
        rows = lax.broadcasted_iota(jnp.int32, (capacity * BLOCK, lanes), 0)
        allowed = rows < counts_ref[pair] * BLOCK
        for k in range(heads_kv):
            cut = slice(k * HD, (k + 1) * HD)
            keys = jnp.concatenate([source[s, 0, :, cut] for s in slots], axis=0)
            values = jnp.concatenate([source[s, 1, :, cut] for s in slots], axis=0)
            update(i, k, keys, values, allowed)

    def clear(i, carry):
        acc[i] = jnp.zeros(acc.shape[1:], jnp.float32)
        stat[i, :heads_kv, :] = jnp.full((heads_kv, lanes), FLOOR, jnp.float32)
        stat[i, heads_kv:, :] = jnp.zeros((heads_kv, lanes), jnp.float32)
        return carry

    lax.fori_loop(0, planes, clear, 0)

    rows = lax.broadcasted_iota(jnp.int32, (tokens, lanes), 0)
    cols = lax.broadcasted_iota(jnp.int32, (tokens, lanes), 1)
    causal = rows <= cols % tokens
    for k in range(heads_kv):
        cut = slice(k * HD, (k + 1) * HD)
        update(0, k, new_ref[0, :, cut], new_ref[1, :, cut], causal)

    def arrived(i, carry):
        @pl.when(i > 0)
        def _():
            q_copy(planes - i).wait_recv()
        fold(i, 0)
        return carry

    lax.fori_loop(0, planes, arrived, 0)
    for j in range(1, members):
        kv_copy(members - j).wait_recv()

        def each(step, carry, j=j):
            i = planes - 1 - step
            fold(i, j)
            if j == members - 1:
                @pl.when(i > 0)
                def _():
                    part_out[i] = acc[i].astype(jnp.bfloat16)
                    part_copy(i).start()
                    stat_copy(i).start()
            return carry

        lax.fori_loop(0, planes, each, 0)

    for i in range(1, planes):
        part_copy(planes - i).wait_recv()
        stat_copy(planes - i).wait_recv()
    for k in range(heads_kv):
        maxima = [stat[0, k:k + 1, :]] + [stat_in[i, k:k + 1, :] for i in range(1, planes)]
        highest = functools.reduce(jnp.maximum, maxima)
        scales = [jnp.exp2(m - highest) for m in maxima]
        total = stat[0, heads_kv + k:heads_kv + k + 1, :] * scales[0]
        mixed = acc[0, k] * scales[0]
        for i in range(1, planes):
            total += stat_in[i, heads_kv + k:heads_kv + k + 1, :] * scales[i]
            mixed += part_in[i, k].astype(jnp.float32) * scales[i]
        mixed = mixed / total
        for g in range(PER_GROUP):
            head = k * PER_GROUP + g
            tile = mixed[:, g * tokens:(g + 1) * tokens]
            out_ref[:, head * HD:(head + 1) * HD] = tile.T.astype(jnp.bfloat16)

    for i in range(1, planes):
        q_copy(i).wait_send()
        part_copy(i).wait_send()
        stat_copy(i).wait_send()
    for j in range(1, members):
        kv_copy(j).wait_send()


def local(queries, new_kv, cache, block_owner, block_slot, prefix_blocks, out_weight):
    replicas = lax.axis_size("replica")
    own = lax.axis_index("replica")
    capacity = max(2, MAXB // replicas)
    planes = math.isqrt(replicas)
    members = replicas // planes
    tokens, heads_kv = queries.shape[0], cache.shape[3] // HD
    lanes = PER_GROUP * tokens
    slots, counts = block_tables(
        block_owner, block_slot, prefix_blocks, own, planes, members, capacity)
    part = (planes, heads_kv, HD, lanes)
    stats = (planes, 2 * heads_kv, lanes)
    vmem = pl.BlockSpec(memory_space=pltpu.VMEM)
    smem = pl.BlockSpec(memory_space=pltpu.SMEM)
    pairs = replicas * capacity * BLOCK * heads_kv * lanes
    attended = pl.pallas_call(
        functools.partial(attend_kernel, planes, members, capacity),
        out_shape=jax.ShapeDtypeStruct(queries.shape, jnp.bfloat16),
        in_specs=[smem, smem, vmem, vmem, vmem],
        out_specs=vmem,
        scratch_shapes=[
            pltpu.VMEM((planes, heads_kv, lanes, HD), jnp.bfloat16),
            [pltpu.VMEM(cache.shape, jnp.bfloat16) for _ in range(members - 1)],
            pltpu.VMEM(part, jnp.float32),
            pltpu.VMEM(stats, jnp.float32),
            pltpu.VMEM(part, jnp.bfloat16),
            pltpu.VMEM(part, jnp.bfloat16),
            pltpu.VMEM(stats, jnp.float32),
            pltpu.SemaphoreType.DMA((planes,)),
            pltpu.SemaphoreType.DMA((planes,)),
            pltpu.SemaphoreType.DMA((members,)),
            pltpu.SemaphoreType.DMA((members,)),
            pltpu.SemaphoreType.DMA((planes,)),
            pltpu.SemaphoreType.DMA((planes,)),
            pltpu.SemaphoreType.DMA((planes,)),
            pltpu.SemaphoreType.DMA((planes,)),
        ],
        compiler_params=pltpu.CompilerParams(
            collective_id=0, has_side_effects=True, vmem_limit_bytes=40 * 1024 * 1024),
        cost_estimate=pl.CostEstimate(
            flops=4 * pairs * HD, bytes_accessed=4 * cache.size, transcendentals=pairs),
    )(slots, counts, queries, new_kv, cache)
    return lax.psum_scatter(
        jnp.dot(attended, out_weight, preferred_element_type=jnp.float32).astype(jnp.bfloat16),
        "tensor",
        scatter_dimension=0,
        tiled=True,
    )


def solution(mesh):
    placed = (
        P("replica", "tensor"),
        P(None, "replica", "tensor"),
        P("replica", None, None, "tensor"),
        P(),
        P(),
        P(),
        P("tensor", None),
    )
    return jax.shard_map(
        local, mesh=mesh, in_specs=placed, out_specs=P(("replica", "tensor"), None), check_vma=False
    )
```

time: 344 us -> 152 us (0.44)
  waiting for transfers between devices: 240 us -> 9.96 us
  Pallas kernels: 0 us -> 110 us
  local copies, waits for them, and re-layouts: 43.6 us -> 6.51 us
  matrix products: 30.6 us -> 9.14 us
  starting transfers between devices: 6.79 us -> 0.01 us
  other arithmetic: 7.93 us -> 1.65 us
    all_to_all x1 -> x0, waiting for transfers between devices: 179 us -> none  [local(): lax.all_to_all(picked, 'replica', split_axis=0, concat_axis=0, tiled=True)]
    pallas_call x0 -> x1, Pallas kernels: none -> 110 us  [local(): pl.pallas_call(functools.partial(attend_kernel, planes, members, capacity...]
    reduce_scatter x1, waiting for transfers between devices: 60.9 us -> 9.95 us  [local(): lax.psum_scatter(jnp.dot(attended, out_weight, preferred_element_type=jnp...]
    dot_general x9 -> x1, matrix products: 30.6 us -> 9.14 us  [local(): jnp.dot(attended, out_weight, preferred_element_type=jnp.float32)]
    another operation x2 -> x0, local copies, waits for them, and re-layouts: 13.8 us -> none  [the longest x1 6.93 us: fold_blocks(): key_rows = chosen[:, 0].reshape(key_count, heads_kv, -1)]
    gather x2 -> x3, local copies, waits for them, and re-layouts: 14.2 us -> 3.11 us  [the longest x1 1.3 us: block_tables(): prefix_blocks[rows]]
    all_to_all x1 -> x0, starting transfers between devices: 6.76 us -> none  [local(): lax.all_to_all(picked, 'replica', split_axis=0, concat_axis=0, tiled=True)]
    dynamic_slice x7 -> x0, local copies, waits for them, and re-layouts: 6.23 us -> none  [the longest x6 5.64 us: advance(): value_tile = lax.dynamic_slice_in_dim(value_rows, offset, key_span, 0)]
  transfers between devices with their start and end apart: 2 -> 1, of which waited for: 2 -> 1; matrix products, arithmetic and copies ran while one was open for 2% -> 0% of each run, Pallas kernels for 0% -> 0%
where the time goes in v1:
time: 152 us; the launch traced here: 151 us
  Pallas kernels  110 us (72%)
  between operations  13.4 us (9%)
  waiting for transfers between devices  9.96 us (7%)
  matrix products  9.14 us (6%)
  local copies, waits for them, and re-layouts  6.51 us (4%)
  other arithmetic  1.65 us (1%)
    pallas_call x1, Pallas kernels, local(): pl.pallas_call(functools.partial(attend_kernel, planes, members, capacity...  110 us
    reduce_scatter x1, waiting for transfers between devices, local(): lax.psum_scatter(jnp.dot(attended, out_weight, preferred_element_type=jnp...  9.95 us
    dot_general x1, matrix products, local(): jnp.dot(attended, out_weight, preferred_element_type=jnp.float32)  9.14 us
    unnamed x8, local copies, waits for them, and re-layouts  3.22 us
  transfers between devices with their start and end apart: 1, of which 1 were waited for; matrix products, arithmetic and copies ran while one was open for 0% of the time, Pallas kernels for 0%

profile of v1, /device:TPU:11, one launch (start us, length us, event | category | flops | bytes accessed | tf_op | source)
XLA Modules:
  0.0 151.1 jit_solution(2403579487505586161)
XLA Ops:
  6.5 0.0 copy-start
  6.5 0.0 reduce-scatter.2.cloned.1.call-start
  6.6 1.3 gather_fusion.1
  7.9 0.1 iota_compare_fusion.1
  8.0 0.0 copy-done
  8.0 0.6 gather_fusion.2
  8.5 1.3 gather_fusion
  9.8 0.2 convert_reduce_fusion
  10.0 0.1 reshape.108.counts_ref
  10.1 1.0 reduce_window_sum.11
  11.0 0.4 select_reduce_fusion
  11.4 0.1 reshape.107.slots_ref
  11.5 0.0 copy-start.1
  11.5 1.2 copy-done.1
  12.7 0.0 copy-start.2
  12.7 1.0 copy-done.2
  13.8 0.0 copy-start.3
  13.8 0.9 copy-done.3
  14.7 110.4 %shard_map.73 = bf16[128,2048]{1,0:T(8,128)(2,1)S(1)} custom-call(s32[64]{0:T(128)S(1)} %reshape.107.slots_ref, s32[16]{0:T(128)S(1)} %reshape.108.counts_ref, bf16[128,2048]{1,0:T(8,128)(2,1)S(1)} %copy-done.2, bf16[2,128,512]{2,1,0:T(8,128)(2,1)S(1)} %copy-done.3, bf16[8,2,64,512]{3,2,1,0:T(8,128)(2,1)S(1)} %copy-done.1), custom_call_target="tpu_custom_call" | custom-call | flops 4294967296 | bytes 2097152 | tf_op jit(solution)/shard_map/pallas_call | solution.py:198
  125.2 9.1 %convolution_convert_fusion = bf16[128,4096]{1,0:T(8,128)(2,1)} fusion(bf16[128,2048]{1,0:T(8,128)(2,1)S(1)} %shard_map.73, bf16[2048,4096]{1,0:T(8,128)(2,1)} %param.13), kind=kOutput, calls=%fused_computation.3 | convolution fusion | flops 2148007936 | bytes 18350080 | tf_op jit(solution)/shard_map/dot_general | solution.py:226
  134.3 0.0 reduce-scatter.2.cloned.1.call-update
  134.3 9.9 %reduce-scatter.2.cloned.1.call-done = bf16[64,4096]{1,0:T(8,128)(2,1)} async-done(((bf16[128,4096]{1,0:T(8,128)(2,1)}), bf16[64,4096]{1,0:T(8,128)(2,1)}) %reduce-scatter.2.cloned.1.call-update) | async-done | bytes 524304 | tf_op jit(solution)/shard_map/reduce_scatter | solution.py:225
  (5 shorter events, 0.0 us)
Async XLA Ops:
  6.5 1.4 copy-start
  6.5 137.7 %reduce-scatter.2.cloned.1.call-start = ((), (), s32[]{:S(2)}) async-start(), calls=%async_computation.1 | async-start | bytes 1572864 | tf_op jit(solution)/shard_map/reduce_scatter | solution.py:225
  11.5 1.2 copy-start.1
  12.7 1.0 copy-start.2
  13.8 0.9 copy-start.3
Sparse Core Ops, SparseCore 0:
  134.4 9.7 reduce-scatter.1

commit v2 on v1

--- a/solution.py
+++ b/solution.py
@@ -22,8 +22,9 @@
 
 def block_tables(block_owner, block_slot, prefix_blocks, own, planes, members, capacity):
     plane, member = own // members, own % members
-    rows = ((plane + jnp.arange(planes, dtype=jnp.int32)) % planes) * members + member
-    owners = plane * members + (member + jnp.arange(members, dtype=jnp.int32)) % members
+    rows = jnp.arange(planes, dtype=jnp.int32) * members + member
+    owners = plane * members + jnp.stack(
+        [plane_peer(member, j, members) for j in range(members)])
     places = jnp.arange(block_owner.shape[1], dtype=jnp.int32)
     owner_rows, slot_rows, lengths = block_owner[rows], block_slot[rows], prefix_blocks[rows]
     used = places[None, :] < lengths[:, None]
@@ -33,6 +34,13 @@
     matches = chosen[:, :, None, :] & (ranks[:, :, None, :] == levels[None, None, :, None])
     slots = jnp.sum(jnp.where(matches, slot_rows[:, None, None, :], 0), axis=3)
     return slots.reshape(-1), jnp.sum(chosen.astype(jnp.int32), axis=2).reshape(-1)
+
+
+def plane_peer(member, j, members):
+    if members == 4:
+        x, y = member % 2, member // 2
+        return member + (j % 2) * (1 - 2 * x) + (j // 2) * (2 - 4 * y)
+    return (member + j) % members
 
 
 def attend_kernel(
@@ -45,46 +53,64 @@
     heads_kv, lanes = acc.shape[1], acc.shape[3]
     tokens = lanes // PER_GROUP
     factor = HD ** (-0.5) * math.log2(math.e)
-
-    def column(i):
-        return {"replica": lax.rem(plane + i, planes) * members + member}
+    square = members == 4
+    last = members - 1
+
+    def beside(way):
+        return {"replica": lax.rem(plane + planes + 2 * way - 1, planes) * members + member}
 
     def in_plane(j):
-        return {"replica": plane * members + lax.rem(member + j, members)}
-
-    def q_copy(i):
-        return pltpu.make_async_remote_copy(
-            qbuf.at[0], qbuf.at[planes - i], q_send.at[i], q_recv.at[planes - i],
-            device_id=column(i), device_id_type=MESH)
+        return {"replica": plane * members + plane_peer(member, j, members)}
+
+    def back(j):
+        return j if square else members - j
+
+    def q_copy(way, origin):
+        return pltpu.make_async_remote_copy(
+            qbuf.at[origin], qbuf.at[origin], q_send.at[way, origin], q_recv.at[origin],
+            device_id=beside(way), device_id_type=MESH)
 
     def kv_copy(j):
         return pltpu.make_async_remote_copy(
-            cache_ref, kvbuf[members - j - 1], kv_send.at[j], kv_recv.at[members - j],
+            cache_ref, kvbuf[back(j) - 1], kv_send.at[j], kv_recv.at[back(j)],
             device_id=in_plane(j), device_id_type=MESH)
 
-    def part_copy(i):
-        return pltpu.make_async_remote_copy(
-            part_out.at[i], part_in.at[planes - i], p_send.at[i], p_recv.at[planes - i],
-            device_id=column(i), device_id_type=MESH)
-
-    def stat_copy(i):
-        return pltpu.make_async_remote_copy(
-            stat.at[i], stat_in.at[planes - i], s_send.at[i], s_recv.at[planes - i],
-            device_id=column(i), device_id_type=MESH)
+    def corner_copy(half):
+        via = kvbuf[1 - half]
+        return pltpu.make_async_remote_copy(
+            via.at[:, half], kvbuf[2].at[:, half], kv_send.at[3 + half], kv_recv.at[3 + half],
+            device_id=in_plane(1 + half), device_id_type=MESH)
+
+    def part_copy(way, target):
+        return pltpu.make_async_remote_copy(
+            part_out.at[target], part_in.at[way, target], p_send.at[target],
+            p_recv.at[way, target],
+            device_id=beside(way), device_id_type=MESH)
+
+    def stat_copy(way, target):
+        return pltpu.make_async_remote_copy(
+            stat.at[target], stat_in.at[way, target], s_send.at[target], s_recv.at[way, target],
+            device_id=beside(way), device_id_type=MESH)
+
+    def has_next(way):
+        return plane > 0 if way == 0 else plane < planes - 1
 
     barrier = pltpu.get_barrier_semaphore()
     for i in range(1, planes):
-        pl.semaphore_signal(barrier, inc=1, device_id=column(i), device_id_type=MESH)
+        column = {"replica": lax.rem(plane + i, planes) * members + member}
+        pl.semaphore_signal(barrier, inc=1, device_id=column, device_id_type=MESH)
     for j in range(1, members):
         pl.semaphore_signal(barrier, inc=1, device_id=in_plane(j), device_id_type=MESH)
     for head in range(heads_kv * PER_GROUP):
         k, g = divmod(head, PER_GROUP)
-        qbuf[0, k, g * tokens:(g + 1) * tokens, :] = q_ref[:, head * HD:(head + 1) * HD]
+        qbuf[plane, k, g * tokens:(g + 1) * tokens, :] = q_ref[:, head * HD:(head + 1) * HD]
     pl.semaphore_wait(barrier, planes + members - 2)
 
-    for i in range(1, planes):
-        q_copy(i).start()
-    for j in range(1, members):
+    for way in range(2):
+        @pl.when(has_next(way))
+        def _(way=way):
+            q_copy(way, plane).start()
+    for j in range(1, members - 1 if square else members):
         kv_copy(j).start()
 
     def update(i, k, keys, values, allowed):
@@ -115,6 +141,16 @@
             values = jnp.concatenate([source[s, 1, :, cut] for s in slots], axis=0)
             update(i, k, keys, values, allowed)
 
+    def merge(way, i):
+        for k in range(heads_kv):
+            here, there = stat[i, k:k + 1, :], stat_in[way, i, k:k + 1, :]
+            highest = jnp.maximum(here, there)
+            mine, other = jnp.exp2(here - highest), jnp.exp2(there - highest)
+            row = slice(heads_kv + k, heads_kv + k + 1)
+            stat[i, row, :] = stat[i, row, :] * mine + stat_in[way, i, row, :] * other
+            stat[i, k:k + 1, :] = highest
+            acc[i, k] = acc[i, k] * mine + part_in[way, i, k].astype(jnp.float32) * other
+
     def clear(i, carry):
         acc[i] = jnp.zeros(acc.shape[1:], jnp.float32)
         stat[i, :heads_kv, :] = jnp.full((heads_kv, lanes), FLOOR, jnp.float32)
@@ -128,56 +164,125 @@
     causal = rows <= cols % tokens
     for k in range(heads_kv):
         cut = slice(k * HD, (k + 1) * HD)
-        update(0, k, new_ref[0, :, cut], new_ref[1, :, cut], causal)
-
-    def arrived(i, carry):
-        @pl.when(i > 0)
+        update(plane, k, new_ref[0, :, cut], new_ref[1, :, cut], causal)
+    fold(plane, 0)
+
+    def pass_queries(distance):
+        for way in range(2):
+            origin = plane + distance * (1 - 2 * way)
+
+            @pl.when((origin >= 0) & (origin < planes))
+            def _(way=way, origin=origin):
+                q_copy(way, origin).wait_recv()
+
+                @pl.when(has_next(way))
+                def _():
+                    q_copy(way, origin).start()
+
+    def near(distance, js):
+        def side(t, carry):
+            origin = plane + distance * (1 - 2 * t)
+
+            @pl.when((origin >= 0) & (origin < planes))
+            def _():
+                for j in js:
+                    fold(origin, j)
+            return carry
+        lax.fori_loop(0, 2, side, 0)
+
+    early = range(1, last)
+    pass_queries(1)
+    near(1, (0,))
+    for j in early:
+        kv_copy(back(j)).wait_recv()
+    if square:
+        for half in range(2):
+            corner_copy(half).start()
+    pass_queries(2)
+
+    def three(t, carry):
+        origin = plane + t - 1
+
+        @pl.when((origin >= 0) & (origin < planes))
         def _():
-            q_copy(planes - i).wait_recv()
-        fold(i, 0)
-        return carry
-
-    lax.fori_loop(0, planes, arrived, 0)
-    for j in range(1, members):
-        kv_copy(members - j).wait_recv()
-
-        def each(step, carry, j=j):
-            i = planes - 1 - step
-            fold(i, j)
-            if j == members - 1:
-                @pl.when(i > 0)
+            for j in early:
+                fold(origin, j)
+        return carry
+
+    lax.fori_loop(0, 3, three, 0)
+
+    def far(distance, carry):
+        @pl.when(distance > 2)
+        def _():
+            pass_queries(distance)
+        near(distance, (0, *early))
+        return carry
+
+    lax.fori_loop(2, planes, far, 0)
+
+    if square:
+        for half in range(2):
+            corner_copy(half).wait_recv()
+    else:
+        kv_copy(back(last)).wait_recv()
+
+    def give(step, carry):
+        for way in range(2):
+            behind = planes - 1 - plane if way == 0 else plane
+            rank = step - behind
+            target = rank if way == 0 else planes - 1 - rank
+            beyond = target < plane if way == 0 else target > plane
+
+            @pl.when((rank >= 0) & beyond)
+            def _(way=way, target=target, behind=behind):
+                fold(target, last)
+
+                @pl.when(behind > 0)
                 def _():
-                    part_out[i] = acc[i].astype(jnp.bfloat16)
-                    part_copy(i).start()
-                    stat_copy(i).start()
-            return carry
-
-        lax.fori_loop(0, planes, each, 0)
-
-    for i in range(1, planes):
-        part_copy(planes - i).wait_recv()
-        stat_copy(planes - i).wait_recv()
+                    part_copy(way, target).wait_recv()
+                    stat_copy(way, target).wait_recv()
+                    merge(way, target)
+                part_out[target] = acc[target].astype(jnp.bfloat16)
+                part_copy(way, target).start()
+                stat_copy(way, target).start()
+        return carry
+
+    lax.fori_loop(0, planes - 1, give, 0)
+    fold(plane, last)
+    for way in range(2):
+        @pl.when(has_next(1 - way))
+        def _(way=way):
+            part_copy(way, plane).wait_recv()
+            stat_copy(way, plane).wait_recv()
+            merge(way, plane)
+
     for k in range(heads_kv):
-        maxima = [stat[0, k:k + 1, :]] + [stat_in[i, k:k + 1, :] for i in range(1, planes)]
-        highest = functools.reduce(jnp.maximum, maxima)
-        scales = [jnp.exp2(m - highest) for m in maxima]
-        total = stat[0, heads_kv + k:heads_kv + k + 1, :] * scales[0]
-        mixed = acc[0, k] * scales[0]
-        for i in range(1, planes):
-            total += stat_in[i, heads_kv + k:heads_kv + k + 1, :] * scales[i]
-            mixed += part_in[i, k].astype(jnp.float32) * scales[i]
-        mixed = mixed / total
+        mixed = acc[plane, k] / stat[plane, heads_kv + k:heads_kv + k + 1, :]
         for g in range(PER_GROUP):
             head = k * PER_GROUP + g
             tile = mixed[:, g * tokens:(g + 1) * tokens]
             out_ref[:, head * HD:(head + 1) * HD] = tile.T.astype(jnp.bfloat16)
 
-    for i in range(1, planes):
-        q_copy(i).wait_send()
-        part_copy(i).wait_send()
-        stat_copy(i).wait_send()
-    for j in range(1, members):
+    def sent(i, carry):
+        for way in range(2):
+            passed = i >= plane if way == 0 else i <= plane
+
+            @pl.when(passed & has_next(way))
+            def _(way=way):
+                q_copy(way, i).wait_send()
+
+        @pl.when(i != plane)
+        def _():
+            part_copy(0, i).wait_send()
+            stat_copy(0, i).wait_send()
+        return carry
+
+    lax.fori_loop(0, planes, sent, 0)
+    for j in range(1, members - 1 if square else members):
         kv_copy(j).wait_send()
+    if square:
+        for half in range(2):
+            corner_copy(half).wait_send()
 
 
 def local(queries, new_kv, cache, block_owner, block_slot, prefix_blocks, out_weight):
@@ -206,16 +311,16 @@
             pltpu.VMEM(part, jnp.float32),
             pltpu.VMEM(stats, jnp.float32),
             pltpu.VMEM(part, jnp.bfloat16),
-            pltpu.VMEM(part, jnp.bfloat16),
-            pltpu.VMEM(stats, jnp.float32),
+            pltpu.VMEM((2, *part), jnp.bfloat16),
+            pltpu.VMEM((2, *stats), jnp.float32),
+            pltpu.SemaphoreType.DMA((2, planes)),
             pltpu.SemaphoreType.DMA((planes,)),
+            pltpu.SemaphoreType.DMA((members + 1,)),
+            pltpu.SemaphoreType.DMA((members + 1,)),
             pltpu.SemaphoreType.DMA((planes,)),
-            pltpu.SemaphoreType.DMA((members,)),
-            pltpu.SemaphoreType.DMA((members,)),
+            pltpu.SemaphoreType.DMA((2, planes)),
             pltpu.SemaphoreType.DMA((planes,)),
-            pltpu.SemaphoreType.DMA((planes,)),
-            pltpu.SemaphoreType.DMA((planes,)),
-            pltpu.SemaphoreType.DMA((planes,)),
+            pltpu.SemaphoreType.DMA((2, planes)),
         ],
         compiler_params=pltpu.CompilerParams(
             collective_id=0, has_side_effects=True, vmem_limit_bytes=40 * 1024 * 1024),

time: 152 us -> 124 us (0.82)
  Pallas kernels: 110 us -> 78.1 us
  waiting for transfers between devices: 9.96 us -> 13.6 us
    pallas_call x1, Pallas kernels: 110 us -> 78.1 us  [local(): pl.pallas_call(functools.partial(attend_kernel, planes, members, capacity...]
    reduce_scatter x1, waiting for transfers between devices: 9.95 us -> 13.6 us  [local(): lax.psum_scatter(jnp.dot(attended, out_weight, preferred_element_type=jnp...]
where the time goes in v2:
time: 124 us; the launch traced here: 123 us
  Pallas kernels  78.1 us (63%)
  waiting for transfers between devices  13.6 us (11%)
  between operations  13.5 us (11%)
  matrix products  9.14 us (7%)
  local copies, waits for them, and re-layouts  6.51 us (5%)
  other arithmetic  1.71 us (1%)
    pallas_call x1, Pallas kernels, local(): pl.pallas_call(functools.partial(attend_kernel, planes, members, capacity...  78.1 us
    reduce_scatter x1, waiting for transfers between devices, local(): lax.psum_scatter(jnp.dot(attended, out_weight, preferred_element_type=jnp...  13.6 us
    dot_general x1, matrix products, local(): jnp.dot(attended, out_weight, preferred_element_type=jnp.float32)  9.14 us
    unnamed x8, local copies, waits for them, and re-layouts  3.22 us
  transfers between devices with their start and end apart: 1, of which 1 were waited for; matrix products, arithmetic and copies ran while one was open for 0% of the time, Pallas kernels for 0%

profile of v2, /device:TPU:11, one launch (start us, length us, event | category | flops | bytes accessed | tf_op | source)
XLA Modules:
  0.0 122.5 jit_solution(348940949918252782)
XLA Ops:
  6.5 0.0 copy-start
  6.5 0.0 reduce-scatter.2.cloned.1.call-start
  6.6 1.3 %gather_fusion.1 = s32[4]{0:T(128)S(1)} fusion(s32[16]{0:T(128)} %param.12, s32[1024]{0:T(1024)S(1)} %pad_clamp_fusion), kind=kCustom, calls=%fused_computation.1 | custom fusion | bytes 48 | tf_op jit(solution)/shard_map/gather | solution.py:29
  7.9 0.1 iota_compare_fusion.1
  8.0 0.0 copy-done
  8.0 0.6 gather_fusion.2
  8.5 1.3 %gather_fusion = s32[4,64]{1,0:T(4,128)S(1)} fusion(s32[16,64]{1,0:T(8,128)} %param.10, s32[1024]{0:T(1024)S(1)} %pad_clamp_fusion), kind=kCustom, calls=%fused_computation | custom fusion | bytes 2064 | tf_op jit(solution)/shard_map/gather | solution.py:29
  9.8 0.1 add_add_fusion
  9.9 0.2 convert_reduce_fusion
  10.1 0.1 reshape.89.counts_ref
  10.2 1.0 reduce_window_sum.11
  11.1 0.4 select_reduce_fusion
  11.5 0.1 reshape.88.slots_ref
  11.6 0.0 copy-start.1
  11.6 1.2 copy-done.1
  12.8 0.0 copy-start.2
  12.8 1.0 copy-done.2
  13.9 0.0 copy-start.3
  13.9 0.9 copy-done.3
  14.8 78.1 %shard_map.73 = bf16[128,2048]{1,0:T(8,128)(2,1)S(1)} custom-call(s32[64]{0:T(128)S(1)} %reshape.88.slots_ref, s32[16]{0:T(128)S(1)} %reshape.89.counts_ref, bf16[128,2048]{1,0:T(8,128)(2,1)S(1)} %copy-done.2, bf16[2,128,512]{2,1,0:T(8,128)(2,1)S(1)} %copy-done.3, bf16[8,2,64,512]{3,2,1,0:T(8,128)(2,1)S(1)} %copy-done.1), custom_call_target="tpu_custom_call" | custom-call | flops 4294967296 | bytes 2097152 | tf_op jit(solution)/shard_map/pallas_call | solution.py:303
  92.9 9.1 %convolution_convert_fusion = bf16[128,4096]{1,0:T(8,128)(2,1)} fusion(bf16[128,2048]{1,0:T(8,128)(2,1)S(1)} %shard_map.73, bf16[2048,4096]{1,0:T(8,128)(2,1)} %param.13), kind=kOutput, calls=%fused_computation.3 | convolution fusion | flops 2148007936 | bytes 18350080 | tf_op jit(solution)/shard_map/dot_general | solution.py:331
  102.1 0.0 reduce-scatter.2.cloned.1.call-update
  102.1 13.6 %reduce-scatter.2.cloned.1.call-done = bf16[64,4096]{1,0:T(8,128)(2,1)} async-done(((bf16[128,4096]{1,0:T(8,128)(2,1)}), bf16[64,4096]{1,0:T(8,128)(2,1)}) %reduce-scatter.2.cloned.1.call-update) | async-done | bytes 524304 | tf_op jit(solution)/shard_map/reduce_scatter | solution.py:330
  (4 shorter events, 0.0 us)
Async XLA Ops:
  6.5 1.5 %copy-start = (s32[16,64]{1,0:T(8,128)S(1)}, s32[16,64]{1,0:T(8,128)}, u32[]{:S(2)}) copy-start(s32[16,64]{1,0:T(8,128)} %param.11) | copy-start | bytes 12292
  6.5 109.2 %reduce-scatter.2.cloned.1.call-start = ((), (), s32[]{:S(2)}) async-start(), calls=%async_computation.1 | async-start | bytes 1572864 | tf_op jit(solution)/shard_map/reduce_scatter | solution.py:330
  11.6 1.2 %copy-start.1 = (bf16[8,2,64,512]{3,2,1,0:T(8,128)(2,1)S(1)}, bf16[8,2,64,512]{3,2,1,0:T(8,128)(2,1)}, u32[]{:S(2)}) copy-start(bf16[8,2,64,512]{3,2,1,0:T(8,128)(2,1)} %cache_ref.1) | copy-start | bytes 3145732
  12.8 1.0 copy-start.2
  13.9 0.9 copy-start.3
Sparse Core Ops, SparseCore 0:
  102.2 13.4 reduce-scatter.1

commit v3 on v2

--- a/solution.py
+++ b/solution.py
@@ -22,14 +22,17 @@
 
 def block_tables(block_owner, block_slot, prefix_blocks, own, planes, members, capacity):
     plane, member = own // members, own % members
-    rows = jnp.arange(planes, dtype=jnp.int32) * members + member
     owners = plane * members + jnp.stack(
         [plane_peer(member, j, members) for j in range(members)])
     places = jnp.arange(block_owner.shape[1], dtype=jnp.int32)
-    owner_rows, slot_rows, lengths = block_owner[rows], block_slot[rows], prefix_blocks[rows]
+    owner_rows, slot_rows, lengths = [
+        lax.dynamic_index_in_dim(
+            table.reshape(planes, members, *table.shape[1:]), member, 1, keepdims=False)
+        for table in (block_owner, block_slot, prefix_blocks)]
     used = places[None, :] < lengths[:, None]
     chosen = (owner_rows[:, None, :] == owners[None, :, None]) & used[:, None, :]
-    ranks = jnp.cumsum(chosen.astype(jnp.int32), axis=2) - 1
+    earlier = places[None, :] < places[:, None]
+    ranks = jnp.sum((chosen[:, :, None, :] & earlier).astype(jnp.int32), axis=3)
     levels = jnp.arange(capacity, dtype=jnp.int32)
     matches = chosen[:, :, None, :] & (ranks[:, :, None, :] == levels[None, None, :, None])
     slots = jnp.sum(jnp.where(matches, slot_rows[:, None, None, :], 0), axis=3)
@@ -44,7 +47,8 @@
 
 
 def attend_kernel(
-    planes, members, capacity, slots_ref, counts_ref, q_ref, new_ref, cache_ref, out_ref,
+    planes, members, capacity, slots_ref, counts_ref, q_hbm, new_hbm, cache_hbm, weight_hbm, out_ref,
+    q_ref, new_ref, cache_ref, weight_ref, attended, mine, theirs, in_sem, y_send, y_recv,
     qbuf, kvbuf, acc, stat, part_out, part_in, stat_in,
     q_send, q_recv, kv_send, kv_recv, p_send, p_recv, s_send, s_recv,
 ):
@@ -72,7 +76,7 @@
 
     def kv_copy(j):
         return pltpu.make_async_remote_copy(
-            cache_ref, kvbuf[back(j) - 1], kv_send.at[j], kv_recv.at[back(j)],
+            cache_hbm, kvbuf[back(j) - 1], kv_send.at[j], kv_recv.at[back(j)],
             device_id=in_plane(j), device_id_type=MESH)
 
     def corner_copy(half):
@@ -95,16 +99,36 @@
     def has_next(way):
         return plane > 0 if way == 0 else plane < planes - 1
 
+    tensors, rank_t = lax.axis_size("tensor"), lax.axis_index("tensor")
+    tiles, tile_rows, tile_cols = mine.shape[1:]
+
+    def y_copy(k, tile):
+        target = lax.rem(rank_t + k, tensors)
+        return pltpu.make_async_remote_copy(
+            mine.at[target, tile], theirs.at[tensors - k, tile],
+            y_send.at[k, tile], y_recv.at[tensors - k, tile],
+            device_id={"tensor": target}, device_id_type=MESH)
+
+    loads = [
+        pltpu.make_async_copy(source, place, in_sem.at[n]) for n, (source, place) in enumerate(
+            ((q_hbm, q_ref), (new_hbm, new_ref), (cache_hbm, cache_ref), (weight_hbm, weight_ref)))]
+    for load in loads[:3]:
+        load.start()
+
     barrier = pltpu.get_barrier_semaphore()
+    for k in range(1, tensors):
+        pl.semaphore_signal(
+            barrier, inc=1, device_id={"tensor": lax.rem(rank_t + k, tensors)}, device_id_type=MESH)
     for i in range(1, planes):
         column = {"replica": lax.rem(plane + i, planes) * members + member}
         pl.semaphore_signal(barrier, inc=1, device_id=column, device_id_type=MESH)
     for j in range(1, members):
         pl.semaphore_signal(barrier, inc=1, device_id=in_plane(j), device_id_type=MESH)
+    loads[0].wait()
     for head in range(heads_kv * PER_GROUP):
         k, g = divmod(head, PER_GROUP)
         qbuf[plane, k, g * tokens:(g + 1) * tokens, :] = q_ref[:, head * HD:(head + 1) * HD]
-    pl.semaphore_wait(barrier, planes + members - 2)
+    pl.semaphore_wait(barrier, planes + members + tensors - 3)
 
     for way in range(2):
         @pl.when(has_next(way))
@@ -158,6 +182,9 @@
         return carry
 
     lax.fori_loop(0, planes, clear, 0)
+    loads[3].start()
+    loads[1].wait()
+    loads[2].wait()
 
     rows = lax.broadcasted_iota(jnp.int32, (tokens, lanes), 0)
     cols = lax.broadcasted_iota(jnp.int32, (tokens, lanes), 1)
@@ -261,7 +288,35 @@
         for g in range(PER_GROUP):
             head = k * PER_GROUP + g
             tile = mixed[:, g * tokens:(g + 1) * tokens]
-            out_ref[:, head * HD:(head + 1) * HD] = tile.T.astype(jnp.bfloat16)
+            attended[:, head * HD:(head + 1) * HD] = tile.T.astype(jnp.bfloat16)
+
+    loads[3].wait()
+
+    def project(tile, carry):
+        cols = pl.ds(pl.multiple_of(tile * tile_cols, tile_cols), tile_cols)
+        product = jnp.dot(
+            attended[...], weight_ref[:, cols], preferred_element_type=jnp.float32)
+        product = product.astype(jnp.bfloat16)
+        for t in range(tensors):
+            mine[t, tile] = product[t * tile_rows:(t + 1) * tile_rows]
+        for k in range(1, tensors):
+            y_copy(k, tile).start()
+        return carry
+
+    lax.fori_loop(0, tiles, project, 0)
+
+    def add_up(tile, carry):
+        cols = pl.ds(pl.multiple_of(tile * tile_cols, tile_cols), tile_cols)
+        total = mine[rank_t, tile].astype(jnp.float32)
+        for k in range(1, tensors):
+            y_copy(tensors - k, tile).wait_recv()
+            total += theirs[k, tile].astype(jnp.float32)
+        out_ref[:, cols] = total.astype(jnp.bfloat16)
+        for k in range(1, tensors):
+            y_copy(k, tile).wait_send()
+        return carry
+
+    lax.fori_loop(0, tiles, add_up, 0)
 
     def sent(i, carry):
         for way in range(2):
@@ -300,12 +355,23 @@
     vmem = pl.BlockSpec(memory_space=pltpu.VMEM)
     smem = pl.BlockSpec(memory_space=pltpu.SMEM)
     pairs = replicas * capacity * BLOCK * heads_kv * lanes
-    attended = pl.pallas_call(
+    tensors, width = lax.axis_size("tensor"), out_weight.shape[1]
+    tile_cols = min(512, width)
+    halves = (tensors, width // tile_cols, tokens // tensors, tile_cols)
+    anywhere = pl.BlockSpec(memory_space=pl.ANY)
+    return pl.pallas_call(
         functools.partial(attend_kernel, planes, members, capacity),
-        out_shape=jax.ShapeDtypeStruct(queries.shape, jnp.bfloat16),
-        in_specs=[smem, smem, vmem, vmem, vmem],
+        out_shape=jax.ShapeDtypeStruct((tokens // tensors, width), jnp.bfloat16),
+        in_specs=[smem, smem, anywhere, anywhere, anywhere, anywhere],
         out_specs=vmem,
         scratch_shapes=[
+            *[pltpu.VMEM(a.shape, jnp.bfloat16) for a in (queries, new_kv, cache, out_weight)],
+            pltpu.VMEM(queries.shape, jnp.bfloat16),
+            pltpu.VMEM(halves, jnp.bfloat16),
+            pltpu.VMEM(halves, jnp.bfloat16),
+            pltpu.SemaphoreType.DMA((4,)),
+            pltpu.SemaphoreType.DMA(halves[:2]),
+            pltpu.SemaphoreType.DMA(halves[:2]),
             pltpu.VMEM((planes, heads_kv, lanes, HD), jnp.bfloat16),
             [pltpu.VMEM(cache.shape, jnp.bfloat16) for _ in range(members - 1)],
             pltpu.VMEM(part, jnp.float32),
@@ -323,16 +389,10 @@
             pltpu.SemaphoreType.DMA((2, planes)),
         ],
         compiler_params=pltpu.CompilerParams(
-            collective_id=0, has_side_effects=True, vmem_limit_bytes=40 * 1024 * 1024),
+            collective_id=0, has_side_effects=True, vmem_limit_bytes=56 * 1024 * 1024),
         cost_estimate=pl.CostEstimate(
-            flops=4 * pairs * HD, bytes_accessed=4 * cache.size, transcendentals=pairs),
-    )(slots, counts, queries, new_kv, cache)
-    return lax.psum_scatter(
-        jnp.dot(attended, out_weight, preferred_element_type=jnp.float32).astype(jnp.bfloat16),
-        "tensor",
-        scatter_dimension=0,
-        tiled=True,
-    )
+            flops=4 * pairs * HD, bytes_accessed=4 * cache.size + 2 * out_weight.size, transcendentals=pairs),
+    )(slots, counts, queries, new_kv, cache, out_weight)
 
 
 def solution(mesh):

time: 124 us -> 94.1 us (0.76)
  waiting for transfers between devices: 13.6 us -> 0 us
  between operations: 13.5 us -> 0.02 us
  Pallas kernels: 78.1 us -> 87.5 us
  matrix products: 9.14 us -> 0 us
  local copies, waits for them, and re-layouts: 6.51 us -> 4.81 us
    reduce_scatter x1 -> x0, waiting for transfers between devices: 13.6 us -> none  [local(): lax.psum_scatter(jnp.dot(attended, out_weight, preferred_element_type=jnp...]
    pallas_call x1, Pallas kernels: 78.1 us -> 87.5 us  [local(): pl.pallas_call(functools.partial(attend_kernel, planes, members, capacity...]
    dot_general x1 -> x0, matrix products: 9.14 us -> none  [local(): jnp.dot(attended, out_weight, preferred_element_type=jnp.float32)]
    gather x3 -> x0, local copies, waits for them, and re-layouts: 3.11 us -> none  [the longest x1 1.3 us: block_tables(): prefix_blocks[rows]]
    unnamed x8 -> x1, local copies, waits for them, and re-layouts: 3.22 us -> 1.87 us
  transfers between devices with their start and end apart: 1 -> 0, of which waited for: 1 -> 0; matrix products, arithmetic and copies ran while one was open for 0% -> 0% of each run, Pallas kernels for 0% -> 0%
where the time goes in v3:
time: 94.1 us; the launch traced here: 93.4 us
  Pallas kernels  87.5 us (93%)
  local copies, waits for them, and re-layouts  4.81 us (5%)
  other arithmetic  1.1 us (1%)
    pallas_call x1, Pallas kernels, local(): pl.pallas_call(functools.partial(attend_kernel, planes, members, capacity...  87.5 us

profile of v3, /device:TPU:11, one launch (start us, length us, event | category | flops | bytes accessed | tf_op | source)
XLA Modules:
  0.0 93.4 jit_solution(12170046074292315920)
XLA Ops:
  0.0 0.1 add_add_fusion
  0.1 0.7 reshape.84
  0.8 0.2 dynamic-slice_reduce_fusion
  1.0 0.1 iota_compare_fusion.2
  1.1 0.7 constant_dynamic-slice_fusion
  1.8 0.2 convert_reduce_fusion.1
  2.0 0.7 reshape.87.counts_ref
  2.7 0.4 convert_reduce_fusion
  3.1 0.4 select_reduce_fusion
  3.4 0.6 reshape.86.slots_ref
  4.1 87.5 %shard_map.73 = bf16[64,4096]{1,0:T(8,128)(2,1)} custom-call(s32[64]{0:T(128)} %reshape.86.slots_ref, s32[16]{0:T(128)} %reshape.87.counts_ref, bf16[128,2048]{1,0:T(8,128)(2,1)} %q_hbm.1, bf16[2,128,512]{2,1,0:T(8,128)(2,1)} %new_hbm.1, bf16[8,2,64,512]{3,2,1,0:T(8,128)(2,1)} %cache_hbm.1, bf16[2048,4096]{1,0:T(8,128)(2,1)} %weight_hbm.1), custom_call_target="tpu_custom_call" | custom-call | flops 4294967296 | bytes 18874368 | tf_op jit(solution)/shard_map/pallas_call | solution.py:362
  91.6 1.9 %copy.9 = bf16[64,4096]{1,0:T(8,128)(2,1)} copy(bf16[64,4096]{1,0:T(8,128)(2,1)} %shard_map.73) | data formatting | bytes 1048576
  (1 shorter events, 0.0 us)

commit v4 on v3

--- a/solution.py
+++ b/solution.py
@@ -85,15 +85,16 @@
             via.at[:, half], kvbuf[2].at[:, half], kv_send.at[3 + half], kv_recv.at[3 + half],
             device_id=in_plane(1 + half), device_id_type=MESH)
 
-    def part_copy(way, target):
-        return pltpu.make_async_remote_copy(
-            part_out.at[target], part_in.at[way, target], p_send.at[target],
-            p_recv.at[way, target],
+    def part_copy(way, target, k):
+        return pltpu.make_async_remote_copy(
+            part_out.at[target, k], part_in.at[way, target, k], p_send.at[target, k],
+            p_recv.at[way, target, k],
             device_id=beside(way), device_id_type=MESH)
 
-    def stat_copy(way, target):
-        return pltpu.make_async_remote_copy(
-            stat.at[target], stat_in.at[way, target], s_send.at[target], s_recv.at[way, target],
+    def stat_copy(way, target, k):
+        return pltpu.make_async_remote_copy(
+            stat.at[target, k], stat_in.at[way, target, k], s_send.at[target, k],
+            s_recv.at[way, target, k],
             device_id=beside(way), device_id_type=MESH)
 
     def has_next(way):
@@ -141,44 +142,45 @@
         scores = lax.dot_general(
             keys, qbuf[i, k], (((1,), (1,)), ((), ())), preferred_element_type=jnp.float32)
         scores = jnp.where(allowed, scores * factor, MASKED)
-        before = stat[i, k:k + 1, :]
+        before = stat[i, k, :1, :]
         highest = jnp.maximum(before, jnp.max(scores, axis=0, keepdims=True))
         weights = jnp.exp2(scores - highest)
         scale = jnp.exp2(before - highest)
-        total = stat[i, heads_kv + k:heads_kv + k + 1, :]
-        stat[i, heads_kv + k:heads_kv + k + 1, :] = (
+        total = stat[i, k, 1:, :]
+        stat[i, k, 1:, :] = (
             total * scale + jnp.sum(weights, axis=0, keepdims=True))
-        stat[i, k:k + 1, :] = highest
+        stat[i, k, :1, :] = highest
         acc[i, k] = acc[i, k] * scale + lax.dot_general(
             values, weights.astype(jnp.bfloat16), (((0,), (0,)), ((), ())),
             preferred_element_type=jnp.float32)
 
-    def fold(i, j):
+    def fold(i, j, heads=range(heads_kv)):
         source = cache_ref if j == 0 else kvbuf[j - 1]
         pair = i * members + j
         slots = [slots_ref[pair * capacity + c] for c in range(capacity)]
         rows = lax.broadcasted_iota(jnp.int32, (capacity * BLOCK, lanes), 0)
         allowed = rows < counts_ref[pair] * BLOCK
-        for k in range(heads_kv):
+        for k in heads:
             cut = slice(k * HD, (k + 1) * HD)
             keys = jnp.concatenate([source[s, 0, :, cut] for s in slots], axis=0)
             values = jnp.concatenate([source[s, 1, :, cut] for s in slots], axis=0)
             update(i, k, keys, values, allowed)
 
-    def merge(way, i):
-        for k in range(heads_kv):
-            here, there = stat[i, k:k + 1, :], stat_in[way, i, k:k + 1, :]
-            highest = jnp.maximum(here, there)
-            mine, other = jnp.exp2(here - highest), jnp.exp2(there - highest)
-            row = slice(heads_kv + k, heads_kv + k + 1)
-            stat[i, row, :] = stat[i, row, :] * mine + stat_in[way, i, row, :] * other
-            stat[i, k:k + 1, :] = highest
-            acc[i, k] = acc[i, k] * mine + part_in[way, i, k].astype(jnp.float32) * other
+    def merge(way, i, k):
+        part_copy(way, i, k).wait_recv()
+        stat_copy(way, i, k).wait_recv()
+        here, there = stat[i, k, :1, :], stat_in[way, i, k, :1, :]
+        highest = jnp.maximum(here, there)
+        mine, other = jnp.exp2(here - highest), jnp.exp2(there - highest)
+        stat[i, k, 1:, :] = stat[i, k, 1:, :] * mine + stat_in[way, i, k, 1:, :] * other
+        stat[i, k, :1, :] = highest
+        acc[i, k] = acc[i, k] * mine + part_in[way, i, k].astype(jnp.float32) * other
 
     def clear(i, carry):
         acc[i] = jnp.zeros(acc.shape[1:], jnp.float32)
-        stat[i, :heads_kv, :] = jnp.full((heads_kv, lanes), FLOOR, jnp.float32)
-        stat[i, heads_kv:, :] = jnp.zeros((heads_kv, lanes), jnp.float32)
+        for k in range(heads_kv):
+            stat[i, k, :1, :] = jnp.full((1, lanes), FLOOR, jnp.float32)
+            stat[i, k, 1:, :] = jnp.zeros((1, lanes), jnp.float32)
         return carry
 
     lax.fori_loop(0, planes, clear, 0)
@@ -262,16 +264,15 @@
 
             @pl.when((rank >= 0) & beyond)
             def _(way=way, target=target, behind=behind):
-                fold(target, last)
-
-                @pl.when(behind > 0)
-                def _():
-                    part_copy(way, target).wait_recv()
-                    stat_copy(way, target).wait_recv()
-                    merge(way, target)
-                part_out[target] = acc[target].astype(jnp.bfloat16)
-                part_copy(way, target).start()
-                stat_copy(way, target).start()
+                for k in range(heads_kv):
+                    fold(target, last, (k,))
+
+                    @pl.when(behind > 0)
+                    def _(k=k):
+                        merge(way, target, k)
+                    part_out[target, k] = acc[target, k].astype(jnp.bfloat16)
+                    part_copy(way, target, k).start()
+                    stat_copy(way, target, k).start()
         return carry
 
     lax.fori_loop(0, planes - 1, give, 0)
@@ -279,12 +280,11 @@
     for way in range(2):
         @pl.when(has_next(1 - way))
         def _(way=way):
-            part_copy(way, plane).wait_recv()
-            stat_copy(way, plane).wait_recv()
-            merge(way, plane)
+            for k in range(heads_kv):
+                merge(way, plane, k)
 
     for k in range(heads_kv):
-        mixed = acc[plane, k] / stat[plane, heads_kv + k:heads_kv + k + 1, :]
+        mixed = acc[plane, k] / stat[plane, k, 1:, :]
         for g in range(PER_GROUP):
             head = k * PER_GROUP + g
             tile = mixed[:, g * tokens:(g + 1) * tokens]
@@ -328,8 +328,9 @@
 
         @pl.when(i != plane)
         def _():
-            part_copy(0, i).wait_send()
-            stat_copy(0, i).wait_send()
+            for k in range(heads_kv):
+                part_copy(0, i, k).wait_send()
+                stat_copy(0, i, k).wait_send()
         return carry
 
     lax.fori_loop(0, planes, sent, 0)
@@ -351,7 +352,7 @@
     slots, counts = block_tables(
         block_owner, block_slot, prefix_blocks, own, planes, members, capacity)
     part = (planes, heads_kv, HD, lanes)
-    stats = (planes, 2 * heads_kv, lanes)
+    stats = (planes, heads_kv, 2, lanes)
     vmem = pl.BlockSpec(memory_space=pltpu.VMEM)
     smem = pl.BlockSpec(memory_space=pltpu.SMEM)
     pairs = replicas * capacity * BLOCK * heads_kv * lanes
@@ -383,10 +384,10 @@
             pltpu.SemaphoreType.DMA((planes,)),
             pltpu.SemaphoreType.DMA((members + 1,)),
             pltpu.SemaphoreType.DMA((members + 1,)),
-            pltpu.SemaphoreType.DMA((planes,)),
-            pltpu.SemaphoreType.DMA((2, planes)),
-            pltpu.SemaphoreType.DMA((planes,)),
-            pltpu.SemaphoreType.DMA((2, planes)),
+            pltpu.SemaphoreType.DMA((planes, heads_kv)),
+            pltpu.SemaphoreType.DMA((2, planes, heads_kv)),
+            pltpu.SemaphoreType.DMA((planes, heads_kv)),
+            pltpu.SemaphoreType.DMA((2, planes, heads_kv)),
         ],
         compiler_params=pltpu.CompilerParams(
             collective_id=0, has_side_effects=True, vmem_limit_bytes=56 * 1024 * 1024),

time: 94.1 us -> 93.3 us (level)
  no operation moved by 1% of the time
where the time goes in v4:
time: 93.3 us; the launch traced here: 93 us
  Pallas kernels  87.1 us (93%)
  local copies, waits for them, and re-layouts  4.81 us (5%)
  other arithmetic  1.1 us (1%)
    pallas_call x1, Pallas kernels, local(): pl.pallas_call(functools.partial(attend_kernel, planes, members, capacity...  87.1 us
    unnamed x1, local copies, waits for them, and re-layouts  1.87 us

profile of v4, /device:TPU:11, one launch (start us, length us, event | category | flops | bytes accessed | tf_op | source)
XLA Modules:
  0.0 93.0 jit_solution(12952497905560422527)
XLA Ops:
  0.0 0.1 add_add_fusion
  0.1 0.7 reshape.84
  0.8 0.2 dynamic-slice_reduce_fusion
  1.0 0.1 iota_compare_fusion.2
  1.1 0.7 constant_dynamic-slice_fusion
  1.8 0.2 convert_reduce_fusion.1
  2.0 0.7 reshape.87.counts_ref
  2.7 0.4 convert_reduce_fusion
  3.1 0.4 select_reduce_fusion
  3.4 0.6 reshape.86.slots_ref
  4.1 87.1 %shard_map.73 = bf16[64,4096]{1,0:T(8,128)(2,1)} custom-call(s32[64]{0:T(128)} %reshape.86.slots_ref, s32[16]{0:T(128)} %reshape.87.counts_ref, bf16[128,2048]{1,0:T(8,128)(2,1)} %q_hbm.1, bf16[2,128,512]{2,1,0:T(8,128)(2,1)} %new_hbm.1, bf16[8,2,64,512]{3,2,1,0:T(8,128)(2,1)} %cache_hbm.1, bf16[2048,4096]{1,0:T(8,128)(2,1)} %weight_hbm.1), custom_call_target="tpu_custom_call" | custom-call | flops 4294967296 | bytes 18874368 | tf_op jit(solution)/shard_map/pallas_call | solution.py:363
  91.1 1.9 %copy.9 = bf16[64,4096]{1,0:T(8,128)(2,1)} copy(bf16[64,4096]{1,0:T(8,128)(2,1)} %shard_map.73) | data formatting | bytes 1048576
  (1 shorter events, 0.0 us)

commit v5 on v4

--- a/solution.py
+++ b/solution.py
@@ -229,16 +229,7 @@
             corner_copy(half).start()
     pass_queries(2)
 
-    def three(t, carry):
-        origin = plane + t - 1
-
-        @pl.when((origin >= 0) & (origin < planes))
-        def _():
-            for j in early:
-                fold(origin, j)
-        return carry
-
-    lax.fori_loop(0, 3, three, 0)
+    near(1, early)
 
     def far(distance, carry):
         @pl.when(distance > 2)
@@ -276,7 +267,8 @@
         return carry
 
     lax.fori_loop(0, planes - 1, give, 0)
-    fold(plane, last)
+    for j in (*early, last):
+        fold(plane, j)
     for way in range(2):
         @pl.when(has_next(1 - way))
         def _(way=way):

time: 93.3 us -> 93.3 us (level)
  no operation moved by 1% of the time
where the time goes in v5:
time: 93.3 us; the launch traced here: 93 us
  Pallas kernels  87.1 us (93%)
  local copies, waits for them, and re-layouts  4.81 us (5%)
  other arithmetic  1.1 us (1%)
    pallas_call x1, Pallas kernels, local(): pl.pallas_call(functools.partial(attend_kernel, planes, members, capacity...  87.1 us
    unnamed x1, local copies, waits for them, and re-layouts  1.87 us

profile of v5, /device:TPU:11, one launch (start us, length us, event | category | flops | bytes accessed | tf_op | source)
XLA Modules:
  0.0 93.0 jit_solution(7491731803090824200)
XLA Ops:
  0.0 0.1 add_add_fusion
  0.1 0.7 reshape.84
  0.8 0.2 dynamic-slice_reduce_fusion
  1.0 0.1 iota_compare_fusion.2
  1.1 0.7 constant_dynamic-slice_fusion
  1.8 0.2 convert_reduce_fusion.1
  2.0 0.7 reshape.87.counts_ref
  2.7 0.4 convert_reduce_fusion
  3.1 0.4 select_reduce_fusion
  3.4 0.6 reshape.86.slots_ref
  4.1 87.1 %shard_map.73 = bf16[64,4096]{1,0:T(8,128)(2,1)} custom-call(s32[64]{0:T(128)} %reshape.86.slots_ref, s32[16]{0:T(128)} %reshape.87.counts_ref, bf16[128,2048]{1,0:T(8,128)(2,1)} %q_hbm.1, bf16[2,128,512]{2,1,0:T(8,128)(2,1)} %new_hbm.1, bf16[8,2,64,512]{3,2,1,0:T(8,128)(2,1)} %cache_hbm.1, bf16[2048,4096]{1,0:T(8,128)(2,1)} %weight_hbm.1), custom_call_target="tpu_custom_call" | custom-call | flops 4294967296 | bytes 18874368 | tf_op jit(solution)/shard_map/pallas_call | solution.py:355
  91.1 1.9 %copy.9 = bf16[64,4096]{1,0:T(8,128)(2,1)} copy(bf16[64,4096]{1,0:T(8,128)(2,1)} %shard_map.73) | data formatting | bytes 1048576
  (1 shorter events, 0.0 us)
